TPU v7x, 32 devices: a whole 2x2x4 slice. The times are simulated.
32 devices in a mesh: blk: 16 (over z, y, core), help: 2 (over x).
Axes of the slice: x: 2, y: 2, z: 4, core: 2. Of those that a mesh axis runs over, the one named last changes fastest.
Arguments:
- heads: float32 [4096, 400], P(('blk', 'help')), may hold values from -6 to 6
- tails: float32 [4096, 400], P(('blk', 'help')), may hold values from -6 to 6
- head_acc: float32 [4096], P(('blk', 'help')), may hold values from 0.01 to 0.1
- tail_acc: float32 [4096], P(('blk', 'help')), may hold values from 0.01 to 0.1
- relations: bfloat16 [7424, 400], replicated, may hold values from -0.59765625 to 0.59765625
- counts: int32 [4, 32], P(None, ('blk', 'help')), may hold values from 1 to 5, as said below
- rel_ids: int32 [4, 32, 5], P(None, ('blk', 'help')), may hold values from 0 to 7423
- head_edges: int32 [4, 32, 5, 1024], P(None, ('blk', 'help')), may hold values from 0 to 127
- tail_edges: int32 [4, 32, 5, 1024], P(None, ('blk', 'help')), may hold values from 0 to 127
Outputs:
- new_heads: float32 [4096, 400], P(('blk', 'help'))
- new_tails: float32 [4096, 400], P(('blk', 'help'))
- new_head_acc: float32 [4096], P(('blk', 'help'))
- new_tail_acc: float32 [4096], P(('blk', 'help'))
Inputs may be any that keep to these rules, and one draw needn't show every extreme that they name: `counts`: in every round the two partitions 2 q and 2 q + 1 have one count from 3 to 5 and the other 1 or 2; in every round partitions 0 and 1 hold 5 and 1.
All inputs are finite; a program needn't handle non-finite values.
Results may differ from a plain program's by a relative error of at most 0.0003.
Values sent between devices are 32-bit elements; how exact they have to be, the bound alone decides.
A program may use at most 64 MiB of HBM per device.

v0:
```python
import jax
import jax.numpy as jnp
from jax import lax
from jax.sharding import PartitionSpec as P

NEG_WEIGHT = 0.0625
LEARN_RATE = 0.1
HIGH = lax.Precision.HIGHEST


def shifted(block, axis, distance):
    devices = range(lax.axis_size(axis))
    route = [((i - distance) % len(devices), i) for i in devices]
    return lax.ppermute(block, axis, route)


def one_hot_rows(index, row_count):
    columns = lax.broadcasted_iota(jnp.int32, (index.shape[0], row_count), 1)
    return (index[:, None] == columns).astype(jnp.bfloat16)


def task_grads(head_block, tail_block, rel_vec, head_index, tail_index):
    row_count = head_block.shape[0]
    scaled = head_block * rel_vec[None, :]
    scores = lax.dot_general(
        scaled,
        tail_block,
        (((1,), (1,)), ((), ())),
        precision=HIGH,
        preferred_element_type=jnp.float32,
    )
    head_hot = one_hot_rows(head_index, row_count)
    tail_hot = one_hot_rows(tail_index, row_count)
    labels = lax.dot_general(
        head_hot, tail_hot, (((0,), (0,)), ((), ())), preferred_element_type=jnp.float32
    )
    coefficient = NEG_WEIGHT * jax.nn.sigmoid(scores) - labels
    head_grad = (
        jnp.dot(coefficient, tail_block, precision=HIGH, preferred_element_type=jnp.float32)
        * rel_vec[None, :]
    )
    tail_grad = lax.dot_general(
        coefficient,
        scaled,
        (((0,), (0,)), ((), ())),
        precision=HIGH,
        preferred_element_type=jnp.float32,
    )
    return (head_grad, tail_grad)


def adagrad(block, state, grad):
    new_state = state + jnp.mean(grad * grad, axis=1)
    return (block - LEARN_RATE * grad / jnp.sqrt(new_state)[:, None], new_state)


def own_grads(head_block, tail_block, relations, counts, rel_ids, head_edges, tail_edges, round_ix):
    rel_row = rel_ids[round_ix, 0]
    head_rows = head_edges[round_ix, 0]
    tail_rows = tail_edges[round_ix, 0]

    def add_task(slot_id, totals):
        rel_vec = relations[rel_row[slot_id]].astype(jnp.float32)
        head_grad, tail_grad = task_grads(
            head_block, tail_block, rel_vec, head_rows[slot_id], tail_rows[slot_id]
        )
        return (totals[0] + head_grad, totals[1] + tail_grad)

    empty = jnp.zeros(head_block.shape, jnp.float32)
    return lax.fori_loop(jnp.int32(0), counts[round_ix, 0], add_task, (empty, empty))


def on_device(heads, tails, head_acc, tail_acc, relations, counts, rel_ids, head_edges, tail_edges):
    rounds_total = counts.shape[0]
    head_block, tail_block, head_state, tail_state = (heads, tails, head_acc, tail_acc)
    for round_ix in range(rounds_total):
        if round_ix > 0:
            tail_block, tail_state = shifted((tail_block, tail_state), "blk", 1)
        head_grad, tail_grad = own_grads(
            head_block, tail_block, relations, counts, rel_ids, head_edges, tail_edges, round_ix
        )
        head_block, head_state = adagrad(head_block, head_state, head_grad)
        tail_block, tail_state = adagrad(tail_block, tail_state, tail_grad)
    tail_block, tail_state = shifted((tail_block, tail_state), "blk", 1 - rounds_total)
    return (head_block, tail_block, head_state, tail_state)


def solution(mesh):
    in_specs = (
        P(("blk", "help"), None),
        P(("blk", "help"), None),
        P(("blk", "help")),
        P(("blk", "help")),
        P(),
        P(None, ("blk", "help")),
        P(None, ("blk", "help"), None),
        P(None, ("blk", "help"), None, None),
        P(None, ("blk", "help"), None, None),
    )
    out_specs = (
        P(("blk", "help"), None),
        P(("blk", "help"), None),
        P(("blk", "help")),
        P(("blk", "help")),
    )
    return jax.shard_map(
        on_device, mesh=mesh, in_specs=in_specs, out_specs=out_specs, check_vma=False
    )
```

profile of v0, /device:TPU:0, one launch (start us, length us, event | category | flops | bytes accessed | tf_op | source)
XLA Modules:
  0.0 171.5 jit_solution(10910555842290120028)
XLA Ops:
  0.7 0.8 fusion.52
  1.5 0.8 fusion.53
  2.3 9.6 %copy.26 = bf16[7424,400]{1,0:T(8,128)(2,1)} copy(bf16[7424,400]{0,1:T(8,128)(2,1)} %param.21) | data formatting | bytes 11878400 | tf_op jit(solution)/shard_map/while | solution.py:70
  12.6 30.3 %while.48 = (s32[]{:T(128)}, f32[128,400]{0,1:T(8,128)S(1)}, f32[128,400]{0,1:T(8,128)S(1)}, s32[]{:T(128)}, s32[5]{0:T(128)S(1)}, /*index=5*/bf16[7424,400]{1,0...) while((s32[]{:T(128)}, f32[128,400]{0,1:T(8,128)S(1)}, ...), condition=%wide.region_1.0_spmd, body=%wide.region_0.0_spmd.sunk | while | flops 270084512 | bytes 1998077 | solution.py:70
  15.6 0.7 dynamic-slice_convert_fusion.8
  16.3 0.7 fusion.109
  17.0 0.6 convolution_subtract_fusion.8
  21.5 0.7 dynamic-slice_convert_fusion.8
  22.2 0.7 fusion.109
  23.0 0.6 convolution_subtract_fusion.8
  27.4 0.7 dynamic-slice_convert_fusion.8
  28.1 0.7 fusion.109
  28.9 0.6 convolution_subtract_fusion.8
  33.4 0.7 dynamic-slice_convert_fusion.8
  34.1 0.7 fusion.109
  34.8 0.6 convolution_subtract_fusion.8
  39.3 0.7 dynamic-slice_convert_fusion.8
  40.0 0.7 fusion.109
  40.8 0.6 convolution_subtract_fusion.8
  43.4 8.6 %collective-permute-done = f32[128,400]{0,1:T(8,128)S(1)} collective-permute-done((f32[128,400]{0,1:T(8,128)S(1)}, f32[128,400]{0,1:T(8,128)S(1)}, u32[]{:S(2)}, u32[]{:S(2)}) %collective-permute-start) | collective-permute-done | bytes 204832 | tf_op jit(solution)/shard_map/ppermute | solution.py:14
  52.2 31.7 %while.49 = (s32[]{:T(128)}, f32[128,400]{0,1:T(8,128)S(1)}, f32[128,400]{0,1:T(8,128)S(1)}, s32[]{:T(128)}, s32[5]{0:T(128)S(1)}, /*index=5*/bf16[7424,400]{1,0...) while((s32[]{:T(128)}, f32[128,400]{0,1:T(8,128)S(1)}, ...), condition=%wide.region_5.0_spmd, body=%wide.region_4.0_spmd.sunk | while | flops 270084512 | bytes 1998077 | solution.py:70
  52.8 0.6 dynamic_slice.77
  55.3 0.7 dynamic-slice_convert_fusion.9
  56.0 0.7 fusion.117
  59.0 0.6 dynamic_slice.77
  61.5 0.7 dynamic-slice_convert_fusion.9
  62.2 0.7 fusion.117
  65.3 0.6 dynamic_slice.77
  67.7 0.7 dynamic-slice_convert_fusion.9
  68.4 0.7 fusion.117
  71.5 0.6 dynamic_slice.77
  73.9 0.7 dynamic-slice_convert_fusion.9
  74.6 0.7 fusion.117
  77.7 0.6 dynamic_slice.77
  80.1 0.7 dynamic-slice_convert_fusion.9
  80.9 0.7 fusion.117
  84.3 7.7 %collective-permute-done.2 = f32[128,400]{0,1:T(8,128)S(1)} collective-permute-done((f32[128,400]{0,1:T(8,128)S(1)}, f32[128,400]{0,1:T(8,128)S(1)}, u32[]{:S(2)}, u32[]{:S(2)}) %collective-permute-start.2) | collective-permute-done | bytes 204832 | tf_op jit(solution)/shard_map/ppermute | solution.py:14
  92.2 32.2 %while.50 = (s32[]{:T(128)}, f32[128,400]{0,1:T(8,128)S(1)}, f32[128,400]{0,1:T(8,128)S(1)}, s32[]{:T(128)}, s32[5]{0:T(128)S(1)}, /*index=5*/bf16[7424,400]{1,0...) while((s32[]{:T(128)}, f32[128,400]{0,1:T(8,128)S(1)}, ...), condition=%wide.region_9.0_spmd, body=%wide.region_8.0_spmd.sunk | while | flops 270084512 | bytes 1998077 | solution.py:70
  95.4 0.7 dynamic-slice_convert_fusion.10
  96.1 0.7 fusion.125
  101.7 0.7 dynamic-slice_convert_fusion.10
  102.4 0.7 fusion.125
  108.0 0.7 dynamic-slice_convert_fusion.10
  108.7 0.7 fusion.125
  114.3 0.7 dynamic-slice_convert_fusion.10
  115.0 0.7 fusion.125
  120.6 0.7 dynamic-slice_convert_fusion.10
  121.3 0.7 fusion.125
  124.8 7.7 %collective-permute-done.4 = f32[128,400]{0,1:T(8,128)S(1)} collective-permute-done((f32[128,400]{0,1:T(8,128)S(1)}, f32[128,400]{0,1:T(8,128)S(1)}, u32[]{:S(2)}, u32[]{:S(2)}) %collective-permute-start.4) | collective-permute-done | bytes 204832 | tf_op jit(solution)/shard_map/ppermute | solution.py:14
  132.6 32.2 %while.51 = (s32[]{:T(128)}, f32[128,400]{0,1:T(8,128)S(1)}, f32[128,400]{0,1:T(8,128)S(1)}, s32[]{:T(128)}, s32[5]{0:T(128)S(1)}, /*index=5*/bf16[7424,400]{1,0...) while((s32[]{:T(128)}, f32[128,400]{0,1:T(8,128)S(1)}, ...), condition=%wide.region_13.0_spmd, body=%wide.region_12.0_spmd.sunk | while | flops 270084512 | bytes 1998077 | solution.py:70
  135.8 0.7 dynamic-slice_convert_fusion.11
  136.5 0.7 fusion.133
  137.3 0.6 convolution_subtract_fusion.11
  142.1 0.7 dynamic-slice_convert_fusion.11
  142.8 0.7 fusion.133
  148.4 0.7 dynamic-slice_convert_fusion.11
  149.2 0.7 fusion.133
  154.8 0.7 dynamic-slice_convert_fusion.11
  155.5 0.7 fusion.133
  161.1 0.7 dynamic-slice_convert_fusion.11
  161.8 0.7 fusion.133
  165.7 0.7 divide_subtract_fusion.1
  166.4 3.9 %collective-permute-done.7 = f32[128]{0:T(128)S(1)} collective-permute-done((f32[128]{0:T(128)S(1)}, f32[128]{0:T(128)S(1)}, u32[]{:S(2)}, u32[]{:S(2)}) %collective-permute-start.7) | collective-permute-done | bytes 544 | tf_op jit(solution)/shard_map/ppermute | solution.py:14
  170.3 0.7 copy.93
  (154 shorter events, 40.9 us)
Async XLA Ops:
  0.6 11.2 %copy-start.2 = (s32[4,1]{0,1:T(1,128)S(1)}, s32[4,1]{0,1:T(1,128)}, u32[]{:S(2)}) copy-start(s32[4,1]{0,1:T(1,128)} %param.22) | copy-start | bytes 52
  0.6 11.8 %copy-start.3 = (s32[4,1,5]{2,1,0:T(1,128)S(1)}, s32[4,1,5]{2,1,0:T(1,128)}, u32[]{:S(2)}) copy-start(s32[4,1,5]{2,1,0:T(1,128)} %param.23) | copy-start | bytes 244
  0.7 11.9 %copy-start.1 = (f32[128,400]{0,1:T(8,128)S(1)}, f32[128,400]{0,1:T(8,128)}, u32[]{:S(2)}) copy-start(f32[128,400]{0,1:T(8,128)} %param.17) | copy-start | bytes 614404
  0.7 11.9 %copy-start = (f32[128,400]{0,1:T(8,128)S(1)}, f32[128,400]{0,1:T(8,128)}, u32[]{:S(2)}) copy-start(f32[128,400]{0,1:T(8,128)} %param.18) | copy-start | bytes 614404
  11.9 31.1 %copy-start.5 = (f32[128]{0:T(128)S(1)}, f32[128]{0:T(128)}, u32[]{:S(2)}) copy-start(f32[128]{0:T(128)} %param.20) | copy-start | bytes 1540
  11.9 31.4 %copy-start.4 = (f32[128]{0:T(128)S(1)}, f32[128]{0:T(128)}, u32[]{:S(2)}) copy-start(f32[128]{0:T(128)} %param.19) | copy-start | bytes 1540
  43.0 8.9 %collective-permute-start = (f32[128,400]{0,1:T(8,128)S(1)}, f32[128,400]{0,1:T(8,128)S(1)}, u32[]{:S(2)}, u32[]{:S(2)}) collective-permute-start(f32[128,400]{0,1:T(8,128)S(1)} %divide_subtract_fusion.6), channel_id=1, source_target_pairs={{30,0},{0,2},{2,4},{4,6},{6,8},{8,10},{10,12},{12,14},{14,16},{16,... | collective-permute-start | bytes 614408 | tf_op jit(solution)/shard_map/ppermute | solution.py:14
  43.1 40.9 %collective-permute-start.1 = (f32[128]{0:T(128)S(1)}, f32[128]{0:T(128)S(1)}, u32[]{:S(2)}, u32[]{:S(2)}) collective-permute-start(f32[128]{0:T(128)S(1)} %get-tuple-element.389), channel_id=1, source_target_pairs={{30,0},{0,2},{2,4},{4,6},{6,8},{8,10},{10,12},{12,14},{14,16},{16,... | collective-permute-start | bytes 1544 | tf_op jit(solution)/shard_map/ppermute | solution.py:14
  84.0 7.9 %collective-permute-start.2 = (f32[128,400]{0,1:T(8,128)S(1)}, f32[128,400]{0,1:T(8,128)S(1)}, u32[]{:S(2)}, u32[]{:S(2)}) collective-permute-start(f32[128,400]{0,1:T(8,128)S(1)} %divide_subtract_fusion.4), channel_id=1, source_target_pairs={{30,0},{0,2},{2,4},{4,6},{6,8},{8,10},{10,12},{12,14},{14,16},{16,... | collective-permute-start | bytes 614408 | tf_op jit(solution)/shard_map/ppermute | solution.py:14
  84.2 40.3 %collective-permute-start.3 = (f32[128]{0:T(128)S(1)}, f32[128]{0:T(128)S(1)}, u32[]{:S(2)}, u32[]{:S(2)}) collective-permute-start(f32[128]{0:T(128)S(1)} %get-tuple-element.385), channel_id=1, source_target_pairs={{30,0},{0,2},{2,4},{4,6},{6,8},{8,10},{10,12},{12,14},{14,16},{16,... | collective-permute-start | bytes 1544 | tf_op jit(solution)/shard_map/ppermute | solution.py:14
  124.5 7.9 %collective-permute-start.4 = (f32[128,400]{0,1:T(8,128)S(1)}, f32[128,400]{0,1:T(8,128)S(1)}, u32[]{:S(2)}, u32[]{:S(2)}) collective-permute-start(f32[128,400]{0,1:T(8,128)S(1)} %divide_subtract_fusion.2), channel_id=1, source_target_pairs={{30,0},{0,2},{2,4},{4,6},{6,8},{8,10},{10,12},{12,14},{14,16},{16,... | collective-permute-start | bytes 614408 | tf_op jit(solution)/shard_map/ppermute | solution.py:14
  124.6 40.3 %collective-permute-start.5 = (f32[128]{0:T(128)S(1)}, f32[128]{0:T(128)S(1)}, u32[]{:S(2)}, u32[]{:S(2)}) collective-permute-start(f32[128]{0:T(128)S(1)} %get-tuple-element.383), channel_id=1, source_target_pairs={{30,0},{0,2},{2,4},{4,6},{6,8},{8,10},{10,12},{12,14},{14,16},{16,... | collective-permute-start | bytes 1544 | tf_op jit(solution)/shard_map/ppermute | solution.py:14
  165.0 5.3 %collective-permute-start.6 = (f32[128,400]{0,1:T(8,128)S(1)}, f32[128,400]{0,1:T(8,128)S(1)}, u32[]{:S(2)}, u32[]{:S(2)}) collective-permute-start(f32[128,400]{0,1:T(8,128)S(1)} %divide_subtract_fusion), channel_id=1, source_target_pairs={{6,0},{8,2},{10,4},{12,6},{14,8},{16,10},{18,12},{20,14},{22,16},{... | collective-permute-start | bytes 614408 | tf_op jit(solution)/shard_map/ppermute | solution.py:14
  165.0 5.2 %collective-permute-start.7 = (f32[128]{0:T(128)S(1)}, f32[128]{0:T(128)S(1)}, u32[]{:S(2)}, u32[]{:S(2)}) collective-permute-start(f32[128]{0:T(128)S(1)} %get-tuple-element.379), channel_id=1, source_target_pairs={{6,0},{8,2},{10,4},{12,6},{14,8},{16,10},{18,12},{20,14},{22,16},{... | collective-permute-start | bytes 1544 | tf_op jit(solution)/shard_map/ppermute | solution.py:14
where the time goes:
time: 173 us; the launch traced here: 171 us
  loops' own time  53.8 us (31%)
  matrix products  46.4 us (27%)
  waiting for transfers between devices  27.9 us (16%)
  local copies, waits for them, and re-layouts  25.8 us (15%)
  other arithmetic  16.2 us (9%)
    another operation x4, loops' own time, own_grads(): lax.fori_loop(jnp.int32(0), counts[round_ix, 0], add_task, (empty, empty))  53.8 us
    ppermute x8, waiting for transfers between devices, shifted(): return lax.ppermute(block, axis, route)  27.9 us
    dot_general x20, matrix products, task_grads(): lax.dot_general(scaled, tail_block, (((1,), (1,)), ((), ())), precision=H...  14.4 us
    mul x20, other arithmetic, task_grads(): scaled = head_block * rel_vec[None, :]  14.1 us
    dot_general x20, matrix products, task_grads(): lax.dot_general(head_hot, tail_hot, (((0,), (0,)), ((), ())), preferred_e...  12.3 us
    dynamic_slice x20, local copies, waits for them, and re-layouts, add_task(): rel_vec = relations[rel_row[slot_id]].astype(jnp.float32)  11.9 us
    dot_general x20, matrix products, task_grads(): jnp.dot(coefficient, tail_block, precision=HIGH, preferred_element_type=j...  11 us
    while x4, local copies, waits for them, and re-layouts, own_grads(): lax.fori_loop(jnp.int32(0), counts[round_ix, 0], add_task, (empty, empty))  9.96 us
  transfers between devices with their start and end apart: 8, of which 4 were waited for; matrix products, arithmetic and copies ran while one was open for 34% of the time, Pallas kernels for 0%

commit v1 on v0

v1 whole, which is shorter than its diff:
```python
import functools

import jax
import jax.numpy as jnp
from jax import lax
from jax.experimental import pallas as pl
from jax.experimental.pallas import tpu as pltpu
from jax.sharding import PartitionSpec as P

NEG_WEIGHT = 0.0625
LEARN_RATE = 0.1
LANES = 128
SUBLANES = 8
NT = (((1,), (1,)), ((), ()))
NN = (((1,), (0,)), ((), ()))


def split(value):
    high = value.astype(jnp.bfloat16)
    return high, (value - high.astype(jnp.float32)).astype(jnp.bfloat16)


def product(left, right, dims):
    def dot(a, b):
        return lax.dot_general(a, b, dims, preferred_element_type=jnp.float32)

    return dot(left[0], right[0]) + (dot(left[0], right[1]) + dot(left[1], right[0]))


def task(s, rows):
    return slice(s * rows, (s + 1) * rows)


def one_hot(index, rows):
    row_of = lax.broadcasted_iota(jnp.int32, (rows, index.shape[1]), 0)
    return jnp.where(row_of == index, 1.0, 0.0).astype(jnp.bfloat16)


def label_counts(head_index, tail_index, rows):
    return lax.dot_general(
        one_hot(tail_index, rows),
        one_hot(head_index, rows),
        NT,
        preferred_element_type=jnp.float32,
    )


def prepare(
    counts_ref,
    rel_ids_ref,
    head_edges_ref,
    tail_edges_ref,
    relations_ref,
    gathered_ref,
    active_ref,
    labels_ref,
    groups,
    sems,
):
    rounds = counts_ref.shape[1]
    slots = rel_ids_ref.shape[2]
    rows = labels_ref.shape[0]
    copies = []
    for at in range(rounds * slots):
        rel_id = rel_ids_ref[at // slots, 0, at % slots]
        start = pl.multiple_of(lax.div(rel_id, LANES) * LANES, LANES)
        copy = pltpu.make_async_copy(
            relations_ref.at[:, pl.ds(start, LANES)], groups.at[at], sems.at[at]
        )
        copy.start()
        copies.append(copy)
    task_of = lax.broadcasted_iota(jnp.int32, (1, slots * rows), 1) // rows
    for k in range(rounds):
        active_ref[k : k + 1, :] = jnp.where(task_of < counts_ref[0, k], 1.0, 0.0)
    for s in range(slots):
        labels_ref[:, task(s, rows)] = label_counts(head_edges_ref[s], tail_edges_ref[s], rows)
    lane_from = lax.broadcasted_iota(jnp.int32, (LANES, LANES), 0)
    lane_to = lax.broadcasted_iota(jnp.int32, (LANES, LANES), 1)
    total = jnp.zeros(gathered_ref.shape, jnp.float32)
    for at, copy in enumerate(copies):
        lane = lax.rem(rel_ids_ref[at // slots, 0, at % slots], LANES)
        pick = jnp.where((lane_from == lane) & (lane_to == at), 1.0, 0.0).astype(jnp.bfloat16)
        copy.wait()
        total = total + jnp.dot(groups[at], pick, preferred_element_type=jnp.float32)
    gathered_ref[...] = total.astype(jnp.bfloat16)


def kernel(
    blk_size,
    slots,
    heads_ref,
    tails_ref,
    head_acc_ref,
    tail_acc_ref,
    head_edges_ref,
    tail_edges_ref,
    gathered_ref,
    active_ref,
    first_labels_ref,
    new_heads_ref,
    new_tails_ref,
    new_head_acc_ref,
    new_tail_acc_ref,
    spread_rel,
    labels,
    scaled_high,
    scaled_low,
    arrived,
    leaving,
    send_sem,
    recv_sem,
):
    width, rows = heads_ref.shape
    rounds = active_ref.shape[0]
    me = lax.axis_index("blk")

    def device(distance):
        return lax.rem(me + distance + blk_size, blk_size)

    barrier = pltpu.get_barrier_semaphore()
    partners = (1, -1, rounds - 1, 1 - rounds)
    for distance in partners:
        pl.semaphore_signal(
            barrier,
            inc=1,
            device_id={"blk": device(distance)},
            device_id_type=pl.DeviceIdType.MESH,
        )

    def store_labels(k):
        for s in range(slots):
            at = k * slots + s
            labels[:, task(s, rows)] = label_counts(head_edges_ref[at], tail_edges_ref[at], rows)

    def store_scaled(k, head_block):
        for s in range(slots):
            lane_of = lax.broadcasted_iota(jnp.int32, (LANES, rows), 0)
            pick = jnp.where(lane_of == k * slots + s, 1.0, 0.0).astype(jnp.bfloat16)
            rel = jnp.dot(gathered_ref[...], pick, preferred_element_type=jnp.float32)
            spread_rel[k % 2, :, task(s, rows)] = rel
            high, low = split(head_block * rel)
            scaled_high[:, task(s, rows)] = high
            scaled_low[:, task(s, rows)] = low

    def adagrad(block, state, grad):
        state = state + jnp.sum(grad * grad, axis=0, keepdims=True) * (1.0 / width)
        return block - grad * (LEARN_RATE / jnp.sqrt(state)), state

    store_scaled(0, heads_ref[...])
    head_state = head_acc_ref[...]
    pl.semaphore_wait(barrier, len(partners))

    copies = []
    for k in range(rounds):
        if k == 0:
            tail_block = tails_ref[...]
            tail_state = tail_acc_ref[...]
        else:
            copies[k - 1].wait_recv()
            tail_block = arrived[k - 1, :width, :]
            tail_state = arrived[k - 1, width : width + 1, :]
        scaled = (scaled_high[...], scaled_low[...])
        scores = product(split(jnp.transpose(tail_block)), scaled, NN)
        active = active_ref[k : k + 1, :]
        counted = first_labels_ref[...] if k == 0 else labels[...]
        weight = active * (0.5 * NEG_WEIGHT)
        coefficient = weight * jnp.tanh(0.5 * scores) + (weight - active * counted)
        coefficient = split(coefficient)
        tail_grad = product(scaled, coefficient, NT)
        new_tail, new_state = adagrad(tail_block, tail_state, tail_grad)
        leaving[k, :width, :] = new_tail
        leaving[k, width:, :] = jnp.broadcast_to(new_state, (SUBLANES, rows))
        copy = pltpu.make_async_remote_copy(
            src_ref=leaving.at[k],
            dst_ref=arrived.at[k],
            send_sem=send_sem.at[k],
            recv_sem=recv_sem.at[k],
            device_id={"blk": device(1 if k < rounds - 1 else 1 - rounds)},
            device_id_type=pl.DeviceIdType.MESH,
        )
        copy.start()
        copies.append(copy)

        weighted = product(split(tail_block), coefficient, NN) * spread_rel[k % 2]
        head_grad = weighted[:, task(0, rows)]
        for s in range(1, slots):
            head_grad = head_grad + weighted[:, task(s, rows)]
        old_head = heads_ref[...] if k == 0 else new_heads_ref[...]
        new_head, head_state = adagrad(old_head, head_state, head_grad)
        new_heads_ref[...] = new_head
        if k < rounds - 1:
            store_scaled(k + 1, new_head)
            store_labels(k + 1)

    new_head_acc_ref[...] = head_state
    copies[-1].wait_recv()
    new_tails_ref[...] = arrived[rounds - 1, :width, :]
    new_tail_acc_ref[...] = arrived[rounds - 1, width : width + 1, :]
    for copy in copies:
        copy.wait_send()


def on_device(
    blk_size, heads, tails, head_acc, tail_acc, relations, counts, rel_ids, head_edges, tail_edges
):
    rows, width = heads.shape
    rounds, _, slots, edges = head_edges.shape
    vmem = pl.BlockSpec(memory_space=pltpu.VMEM)
    smem = pl.BlockSpec(memory_space=pltpu.SMEM)
    head_edges = head_edges.reshape(rounds * slots, 1, edges)
    tail_edges = tail_edges.reshape(rounds * slots, 1, edges)
    gathered, active, first_labels = pl.pallas_call(
        prepare,
        out_shape=(
            jax.ShapeDtypeStruct((width, LANES), jnp.bfloat16),
            jax.ShapeDtypeStruct((rounds, slots * rows), jnp.float32),
            jax.ShapeDtypeStruct((rows, slots * rows), jnp.float32),
        ),
        in_specs=[smem, smem, vmem, vmem, pl.BlockSpec(memory_space=pl.ANY)],
        out_specs=(vmem, vmem, vmem),
        scratch_shapes=[
            pltpu.VMEM((rounds * slots, width, LANES), jnp.bfloat16),
            pltpu.SemaphoreType.DMA((rounds * slots,)),
        ],
        compiler_params=pltpu.CompilerParams(vmem_limit_bytes=24 * 1024 * 1024),
    )(counts.T, rel_ids, head_edges, tail_edges, relations.T)
    new_heads, new_tails, new_head_acc, new_tail_acc = pl.pallas_call(
        functools.partial(kernel, blk_size, slots),
        out_shape=(
            jax.ShapeDtypeStruct((width, rows), jnp.float32),
            jax.ShapeDtypeStruct((width, rows), jnp.float32),
            jax.ShapeDtypeStruct((1, rows), jnp.float32),
            jax.ShapeDtypeStruct((1, rows), jnp.float32),
        ),
        in_specs=[vmem] * 9,
        out_specs=(vmem, vmem, vmem, vmem),
        scratch_shapes=[
            pltpu.VMEM((2, width, slots * rows), jnp.float32),
            pltpu.VMEM((rows, slots * rows), jnp.float32),
            pltpu.VMEM((width, slots * rows), jnp.bfloat16),
            pltpu.VMEM((width, slots * rows), jnp.bfloat16),
            pltpu.VMEM((rounds, width + SUBLANES, rows), jnp.float32),
            pltpu.VMEM((rounds, width + SUBLANES, rows), jnp.float32),
            pltpu.SemaphoreType.DMA((rounds,)),
            pltpu.SemaphoreType.DMA((rounds,)),
        ],
        compiler_params=pltpu.CompilerParams(
            collective_id=0, has_side_effects=True, vmem_limit_bytes=48 * 1024 * 1024
        ),
    )(
        heads.T,
        tails.T,
        head_acc.reshape(1, rows),
        tail_acc.reshape(1, rows),
        head_edges,
        tail_edges,
        gathered,
        active,
        first_labels,
    )
    return (new_heads.T, new_tails.T, new_head_acc.reshape(rows), new_tail_acc.reshape(rows))


def solution(mesh):
    both = ("blk", "help")
    in_specs = (
        P(both, None),
        P(both, None),
        P(both),
        P(both),
        P(),
        P(None, both),
        P(None, both, None),
        P(None, both, None, None),
        P(None, both, None, None),
    )
    out_specs = (P(both, None), P(both, None), P(both), P(both))
    return jax.shard_map(
        functools.partial(on_device, mesh.shape["blk"]),
        mesh=mesh,
        in_specs=in_specs,
        out_specs=out_specs,
        check_vma=False,
    )
```

time: 173 us -> 41.5 us (0.24)
  the two profiles are of different devices: /device:TPU:0 before, /device:TPU:1 now
where the time goes in v1:
time: 41.5 us; the launch traced here: 41.2 us
  Pallas kernels  32.3 us (78%)
  local copies, waits for them, and re-layouts  8.2 us (20%)
  between operations  0.73 us (2%)
    pallas_call x1, Pallas kernels, on_device(): pl.pallas_call(functools.partial(kernel, blk_size, slots), out_shape=(jax...  27.8 us
    unnamed x26, local copies, waits for them, and re-layouts  8.2 us
    pallas_call x1, Pallas kernels, on_device(): pl.pallas_call(prepare, out_shape=(jax.ShapeDtypeStruct((width, LANES), j...  4.53 us

profile of v1, /device:TPU:1, one launch (start us, length us, event | category | flops | bytes accessed | tf_op | source)
XLA Modules:
  0.0 41.2 jit_solution(13148930340046548587)
XLA Ops:
  0.6 0.0 copy-start.10
  0.6 0.0 copy-start.9
  0.7 0.0 copy-start
  0.7 2.7 %copy-done = bf16[7424,400]{0,1:T(8,128)(2,1)S(1)} copy-done((bf16[7424,400]{0,1:T(8,128)(2,1)S(1)}, bf16[7424,400]{0,1:T(8,128)(2,1)}, u32[]{:S(2)}) %copy-start) | copy-done | bytes 5939224
  3.4 0.0 copy-start.1
  3.4 0.9 %copy-done.1 = s32[4,1,5,1024]{3,1,2,0:T(1,128)S(1)} copy-done((s32[4,1,5,1024]{3,1,2,0:T(1,128)S(1)}, s32[4,1,5,1024]{3,1,2,0:T(1,128)}, u32[]{:S(2)}) %copy-start.1) | copy-done | bytes 81944
  4.2 0.0 copy-start.3
  4.2 0.9 %copy-done.3 = s32[4,1,5,1024]{3,1,2,0:T(1,128)S(1)} copy-done((s32[4,1,5,1024]{3,1,2,0:T(1,128)S(1)}, s32[4,1,5,1024]{3,1,2,0:T(1,128)}, u32[]{:S(2)}) %copy-start.3) | copy-done | bytes 81944
  5.1 0.0 copy-start.7
  5.1 0.7 %copy-done.7 = s32[4,1,5]{2,1,0:T(1,128)S(1)} copy-done((s32[4,1,5]{2,1,0:T(1,128)S(1)}, s32[4,1,5]{2,1,0:T(1,128)}, u32[]{:S(2)}) %copy-start.7) | copy-done | bytes 104
  5.8 0.0 copy-start.8
  5.8 0.7 %copy-done.8 = s32[4,1]{0,1:T(1,128)S(1)} copy-done((s32[4,1]{0,1:T(1,128)S(1)}, s32[4,1]{0,1:T(1,128)}, u32[]{:S(2)}) %copy-start.8) | copy-done | bytes 40
  6.5 0.0 copy-start.2
  6.5 0.0 copy-start.4
  6.5 0.0 copy-start.5
  6.5 0.0 copy-start.6
  6.5 4.5 %shard_map.120 = (bf16[400,128]{1,0:T(8,128)(2,1)S(1)}, f32[4,640]{1,0:T(4,128)S(1)}, f32[128,640]{1,0:T(8,128)S(1)}) custom-call(s32[1,4]{1,0:T(1,128)S(1)} %bitcast.21, s32[4,1,5]{2,1,0:T(1,128)S(1)} %copy-done.7, s32[20,1,1024]{2,1,0:T(1,128)S(1)} %bitcast.13, s32[20,1,1024]{2,1,0:T(1,128)S(1)} %bitcast.15, bf16[400,7424]{1,0:T(8,128)(2,1)S(1)} %bitcast.12), custom_call_target="tpu_custom_call" | custom-call | tf_op jit(solution)/shard_map/pallas_call | solution.py:212
  11.0 0.0 copy-done.10
  11.0 0.0 copy-done.9
  11.0 0.0 copy-done.2
  11.0 0.0 copy-done.4
  11.1 0.0 copy-done.5
  11.1 0.0 copy-done.6
  11.1 27.8 %shard_map.121 = (f32[400,128]{1,0:T(8,128)S(1)}, f32[400,128]{1,0:T(8,128)S(1)}, f32[1,128]{1,0:T(1,128)S(1)}, f32[1,128]{1,0:T(1,128)S(1)}) custom-call(f32[400,128]{1,0:T(8,128)S(1)} %bitcast.17, f32[400,128]{1,0:T(8,128)S(1)} %bitcast.18, f32[1,128]{1,0:T(1,128)S(1)} %bitcast.22, f32[1,128]{1,0:T(1,128)S(1)} %bitcast.23, s32[20,1,1024]{2,1,0:T(1,128)S(1)} %bitcast.14, ...), custom_call_target="tpu_custom_call" | custom-call | tf_op jit(solution)/shard_map/pallas_call | solution.py:227
  38.8 0.7 %copy.17 = f32[128,400]{0,1:T(8,128)} copy(f32[128,400]{0,1:T(8,128)S(1)} %bitcast.20) | data formatting | bytes 409600
  39.5 0.7 %copy.18 = f32[128,400]{0,1:T(8,128)} copy(f32[128,400]{0,1:T(8,128)S(1)} %bitcast.19) | data formatting | bytes 409600
  40.2 0.5 %copy.19 = f32[128]{0:T(128)} copy(f32[128]{0:T(128)S(1)} %bitcast.25) | data formatting | bytes 1024
  40.7 0.5 %copy.20 = f32[128]{0:T(128)} copy(f32[128]{0:T(128)S(1)} %bitcast.24) | data formatting | bytes 1024
Async XLA Ops:
  0.6 10.4 %copy-start.10 = (f32[128]{0:T(128)S(1)}, f32[128]{0:T(128)}, u32[]{:S(2)}) copy-start(f32[128]{0:T(128)} %param.12) | copy-start | bytes 1540
  0.6 10.4 %copy-start.9 = (f32[128]{0:T(128)S(1)}, f32[128]{0:T(128)}, u32[]{:S(2)}) copy-start(f32[128]{0:T(128)} %param.11) | copy-start | bytes 1540
  0.7 2.7 %copy-start = (bf16[7424,400]{0,1:T(8,128)(2,1)S(1)}, bf16[7424,400]{0,1:T(8,128)(2,1)}, u32[]{:S(2)}) copy-start(bf16[7424,400]{0,1:T(8,128)(2,1)} %param.13) | copy-start | bytes 17817604
  3.4 0.9 %copy-start.1 = (s32[4,1,5,1024]{3,1,2,0:T(1,128)S(1)}, s32[4,1,5,1024]{3,1,2,0:T(1,128)}, u32[]{:S(2)}) copy-start(s32[4,1,5,1024]{3,1,2,0:T(1,128)} %param.16) | copy-start | bytes 245764
  4.2 0.9 %copy-start.3 = (s32[4,1,5,1024]{3,1,2,0:T(1,128)S(1)}, s32[4,1,5,1024]{3,1,2,0:T(1,128)}, u32[]{:S(2)}) copy-start(s32[4,1,5,1024]{3,1,2,0:T(1,128)} %param.17) | copy-start | bytes 245764
  5.1 0.7 %copy-start.7 = (s32[4,1,5]{2,1,0:T(1,128)S(1)}, s32[4,1,5]{2,1,0:T(1,128)}, u32[]{:S(2)}) copy-start(s32[4,1,5]{2,1,0:T(1,128)} %rel_ids_ref.1) | copy-start | bytes 244
  5.8 0.7 %copy-start.8 = (s32[4,1]{0,1:T(1,128)S(1)}, s32[4,1]{0,1:T(1,128)}, u32[]{:S(2)}) copy-start(s32[4,1]{0,1:T(1,128)} %param.14) | copy-start | bytes 52
  6.5 4.6 %copy-start.2 = (s32[4,1,5,1024]{3,1,2,0:T(1,128)S(1)}, s32[4,1,5,1024]{3,1,2,0:T(1,128)}, u32[]{:S(2)}) copy-start(s32[4,1,5,1024]{3,1,2,0:T(1,128)} %param.16) | copy-start | bytes 245764
  6.5 4.6 %copy-start.4 = (s32[4,1,5,1024]{3,1,2,0:T(1,128)S(1)}, s32[4,1,5,1024]{3,1,2,0:T(1,128)}, u32[]{:S(2)}) copy-start(s32[4,1,5,1024]{3,1,2,0:T(1,128)} %param.17) | copy-start | bytes 245764
  6.5 4.6 %copy-start.5 = (f32[128,400]{0,1:T(8,128)S(1)}, f32[128,400]{0,1:T(8,128)}, u32[]{:S(2)}) copy-start(f32[128,400]{0,1:T(8,128)} %param.9) | copy-start | bytes 614404
  6.5 4.6 %copy-start.6 = (f32[128,400]{0,1:T(8,128)S(1)}, f32[128,400]{0,1:T(8,128)}, u32[]{:S(2)}) copy-start(f32[128,400]{0,1:T(8,128)} %param.10) | copy-start | bytes 614404
